TPU v7x, 32 devices: a whole 2x2x4 slice. The times are simulated.
32 devices in a mesh: plate: 4 (over y, x), sub: 8 (over z, core).
Axes of the slice: x: 2, y: 2, z: 4, core: 2. Of those that a mesh axis runs over, the one named last changes fastest.
Arguments:
- populations: float32 [19, 16, 128, 128], P(None, 'plate', 'sub'), may hold values from 0.5 to 1.5
- solid: int32 [16, 128, 128], P('plate', 'sub'), may hold values 0 or 1
- marker_corner: int32 [3, 2048], P(None, ('plate', 'sub')), may hold values from 0 to 124, as said below
- marker_frac: float32 [3, 2048], P(None, ('plate', 'sub')), may hold values from 0 to 1
- marker_target: float32 [3, 2048], P(None, ('plate', 'sub')), may hold values from -0.6 to 0.6
- stiffness: float32 [2048], P(('plate', 'sub')), may hold values from 0.5 to 4
- displacement: float32 [3, 2048], P(None, ('plate', 'sub')), may hold values from -0.6 to 0.6
Outputs:
- populations_out: float32 [19, 16, 128, 128], P(None, 'plate', 'sub')
- displacement_out: float32 [3, 2048], P(None, ('plate', 'sub'))
- marker_force: float32 [3, 2048], P(None, ('plate', 'sub'))
Inputs may be any that keep to these rules, and one draw needn't show every extreme that they name: `marker_corner`: components are the first cell of the stencil along the three dimensions. Every stencil lies inside the grid without wrapping, and along the first dimension inside the slab of 4 cells that its plate's markers share; the markers of plate p are rows p * 512 to (p + 1) * 512 - 1 and lie in slab p.
All inputs are finite; a program needn't handle non-finite values. No bound on the sum of `solid` on one device may be relied on, other than what follows from the above.
Results may differ from a plain program's by a relative error of at most 0.00011.
Values sent between devices are 32-bit elements; how exact they have to be, the bound alone decides.
A program may use at most 64 MiB of HBM per device.

v0:
```python
import jax
import jax.numpy as jnp
from jax import lax
from jax.sharding import PartitionSpec as P

STEPS = 2


DIRS = [
    (0, 0, 0),
    (1, 0, 0),
    (-1, 0, 0),
    (0, 1, 0),
    (0, -1, 0),
    (0, 0, 1),
    (0, 0, -1),
    (1, 1, 0),
    (-1, -1, 0),
    (1, -1, 0),
    (-1, 1, 0),
    (1, 0, 1),
    (-1, 0, -1),
    (1, 0, -1),
    (-1, 0, 1),
    (0, 1, 1),
    (0, -1, -1),
    (0, 1, -1),
    (0, -1, 1),
]
WEIGHTS = [1.0 / 3.0] + [1.0 / 18.0] * 6 + [1.0 / 36.0] * 12
OPPOSITE = [0, 2, 1, 4, 3, 6, 5, 8, 7, 10, 9, 12, 11, 14, 13, 16, 15, 18, 17]
KAPPA = 4.0
RELAX = 0.9


def extended(x, sides, width):
    for axis, dim in sides:
        peers, length = (lax.axis_size(axis), x.shape[dim])
        up = [(i, (i + 1) % peers) for i in range(peers)]
        down = [(j, i) for i, j in up]
        last = lax.slice_in_dim(x, length - width, length, axis=dim)
        initial = lax.slice_in_dim(x, 0, width, axis=dim)
        before = lax.ppermute(last, axis, up)
        after = lax.ppermute(initial, axis, down)
        x = jnp.concatenate([before, x, after], axis=dim)
    return x


def kernel_weights(frac):
    root = jnp.sqrt(1.0 + 4.0 * frac - 4.0 * frac * frac)
    second = (3.0 - 2.0 * frac + root) / 8.0
    third = (1.0 + 2.0 * frac + root) / 8.0
    return jnp.stack([0.5 - third, second, third, 0.5 - second])


def dense_rows(first, weights, length):
    cells = jnp.arange(length, dtype=jnp.int32)[:, None]
    result = jnp.zeros((length, first.shape[0]), jnp.float32)
    for offset in range(4):
        result = result + weights[offset][None, :] * (cells == (first + offset)[None, :]).astype(
            jnp.float32
        )
    return result


def moments(pops):
    density = jnp.sum(pops, 0)
    comps = []
    for axis in range(3):
        total = jnp.zeros_like(density)
        for index in range(19):
            if DIRS[index][axis] == 1:
                total = total + pops[index]
            elif DIRS[index][axis] == -1:
                total = total - pops[index]
        comps.append(total)
    return (density, jnp.stack(comps) / density)


def dotted(index, vectors):
    total = jnp.zeros_like(vectors[0])
    for axis in range(3):
        if DIRS[index][axis] == 1:
            total = total + vectors[axis]
        elif DIRS[index][axis] == -1:
            total = total - vectors[axis]
    return total


def collide(pops, density, velocity, spread, fluid):
    speed_sq = jnp.sum(velocity * velocity, 0)
    result = []
    for index in range(19):
        proj = dotted(index, velocity)
        equil = WEIGHTS[index] * density * (1.0 + 3.0 * proj + 4.5 * proj * proj - 1.5 * speed_sq)
        post = (
            pops[index]
            - (pops[index] - equil) / RELAX
            + 3.0 * WEIGHTS[index] * dotted(index, spread)
        )
        result.append(jnp.where(fluid, post, pops[OPPOSITE[index]]))
    return jnp.stack(result)


def padded_post(post):
    return extended(post, (("plate", 1), ("sub", 2)), 1)


def stream_cells(padded, size_x, size_y):
    result = []
    for index in range(19):
        shift_x, shift_y, shift_z = DIRS[index]
        moved = padded[
            index, 1 - shift_x : 1 - shift_x + size_x, 1 - shift_y : 1 - shift_y + size_y, :
        ]
        result.append(jnp.roll(moved, shift_z, axis=2))
    return jnp.stack(result)


def shards(populations, solid, marker_corner, marker_frac, marker_target, stiffness, displacement):
    count, size_x, size_y, size_z = populations.shape
    own_count = stiffness.shape[0]
    corners = lax.all_gather(marker_corner, "sub", axis=1, tiled=True)
    fracs = lax.all_gather(marker_frac, "sub", axis=1, tiled=True)
    x_first = corners[0] - lax.axis_index("plate") * size_x
    y_first = corners[1] - lax.axis_index("sub") * size_y
    x_rows = dense_rows(x_first, kernel_weights(fracs[0]), size_x)
    y_rows = dense_rows(y_first, kernel_weights(fracs[1]), size_y)
    z_rows = dense_rows(corners[2], kernel_weights(fracs[2]), size_z)
    plate_count = x_rows.shape[1]
    xy_rows = (x_rows[:, None, :] * y_rows[None, :, :]).reshape(size_x * size_y, plate_count)
    fluid = solid == 0
    stacked = jnp.concatenate([marker_target, stiffness[None], displacement], 0)
    state = lax.all_gather(stacked, "sub", axis=1, tiled=True)
    target_now, spring_now, disp = (state[:3], state[3], state[4:])
    force = jnp.zeros_like(disp)
    pops = populations
    for step in range(STEPS):
        density, velocity = moments(pops)
        flat = velocity.reshape(3, size_x * size_y, size_z)
        along_z = jnp.einsum("kcz,zm->kcm", flat, z_rows, precision=lax.Precision.HIGHEST)
        partial_value = jnp.sum(along_z * xy_rows[None], 1)
        marker_vel = lax.psum(partial_value, "sub")
        force = KAPPA * (target_now - marker_vel) - spring_now[None] * disp
        disp = disp + marker_vel
        weighted = xy_rows[None] * force[:, None, :]
        spread = jnp.einsum("kcm,zm->kcz", weighted, z_rows, precision=lax.Precision.HIGHEST)
        spread = spread.reshape(3, size_x, size_y, size_z)
        post = collide(pops, density, velocity, spread, fluid)
        pops = stream_cells(padded_post(post), size_x, size_y)
    offset = lax.axis_index("sub") * own_count
    disp = lax.dynamic_slice_in_dim(disp, offset, own_count, 1)
    force = lax.dynamic_slice_in_dim(force, offset, own_count, 1)
    return (pops, disp, force)


def solution(mesh):
    in_specs = (
        P(None, "plate", "sub", None),
        P("plate", "sub", None),
        P(None, ("plate", "sub")),
        P(None, ("plate", "sub")),
        P(None, ("plate", "sub")),
        P(("plate", "sub")),
        P(None, ("plate", "sub")),
    )
    out_specs = (
        P(None, "plate", "sub", None),
        P(None, ("plate", "sub")),
        P(None, ("plate", "sub")),
    )
    return jax.shard_map(shards, mesh=mesh, in_specs=in_specs, out_specs=out_specs, check_vma=False)
```

profile of v0, /device:TPU:0, one launch (start us, length us, event | category | flops | bytes accessed | tf_op | source)
XLA Modules:
  0.0 113.2 jit_solution(7539751495723688543)
XLA Ops:
  0.6 1.0 add_subtract_fusion.2
  1.6 0.9 add_subtract_fusion.3
  2.6 0.7 copy-done.3
  3.3 14.4 %all-gather = s32[8,64,3]{1,2,0:T(4,128)S(1)} all-gather(s32[1,64,3]{1,2,0:T(4,128)S(1)} %bitcast.808), channel_id=1, replica_groups=mesh['plate'=4,'sub'=8] {'sub'}, dimensions={0}, use_global_device_ids=true | all-gather | bytes 6912 | tf_op jit(solution)/shard_map/all_gather | solution.py:123
  17.7 0.1 reshape.897
  17.8 0.6 copy-done.4
  18.4 12.7 %all-gather.1 = f32[8,64,3]{1,2,0:T(4,128)S(1)} all-gather(f32[1,64,3]{1,2,0:T(4,128)S(1)} %bitcast.809), channel_id=1, replica_groups=mesh['plate'=4,'sub'=8] {'sub'}, dimensions={0}, use_global_device_ids=true | all-gather | bytes 6912 | tf_op jit(solution)/shard_map/all_gather | solution.py:124
  31.1 0.1 reshape.899
  31.2 0.6 copy-done.5
  31.9 14.0 %all-gather.2 = f32[8,64,7]{1,2,0:T(8,128)S(1)} all-gather(f32[1,64,7]{1,2,0:T(8,128)S(1)} %maximum_bitcast_fusion.18), channel_id=1, replica_groups=mesh['plate'=4,'sub'=8] {'sub'}, dimensions={0}, use_global_device_ids=true | all-gather | bytes 16128 | tf_op jit(solution)/shard_map/all_gather | solution.py:134
  46.2 0.6 fusion
  46.8 14.6 %psum.14 = f32[3,512]{1,0:T(4,128)S(1)} all-reduce(f32[3,512]{1,0:T(4,128)S(1)} %fusion), channel_id=1, replica_groups=mesh['plate'=4,'sub'=8] {'sub'}, use_global_device_ids=true, to_apply=%region_3.0 | all-reduce | flops 1536 | bytes 12288 | tf_op jit(solution)/shard_map/psum | solution.py:143
  61.4 0.6 fusion.4
  62.0 0.7 copy-done.2
  63.5 2.5 %collective-permute-start.1 = (f32[19,1,16,128]{3,2,1,0:T(8,128)S(1)}, f32[19,1,16,128]{3,2,1,0:T(8,128)S(1)}, u32[]{:S(2)}, u32[]{:S(2)}) collective-permute-start(f32[19,1,16,128]{3,2,1,0:T(8,128)S(1)} %get-tuple-element.86), channel_id=1, source_target_pairs={{8,0},{16,8},{24,16},{0,24},{9,1},{17,9},{25,17},{1,25},{10,2},{18... | collective-permute-start | bytes 466952 | tf_op jit(solution)/shard_map/ppermute | solution.py:44
  66.1 4.1 %collective-permute-done.1 = f32[19,1,16,128]{3,2,1,0:T(8,128)S(1)} collective-permute-done((f32[19,1,16,128]{3,2,1,0:T(8,128)S(1)}, f32[19,1,16,128]{3,2,1,0:T(8,128)S(1)}, u32[]{:S(2)}, u32[]{:S(2)}) %collective-permute-start.1) | collective-permute-done | bytes 155680 | tf_op jit(solution)/shard_map/ppermute | solution.py:44
  70.2 2.8 %collective-permute-done = f32[19,1,16,128]{3,2,1,0:T(8,128)S(1)} collective-permute-done((f32[19,1,16,128]{3,2,1,0:T(8,128)S(1)}, f32[19,1,16,128]{3,2,1,0:T(8,128)S(1)}, u32[]{:S(2)}, u32[]{:S(2)}) %collective-permute-start) | collective-permute-done | bytes 155680 | tf_op jit(solution)/shard_map/ppermute | solution.py:43
  73.3 0.1 pad_maximum_fusion.3
  73.5 0.5 collective-permute-start.2
  74.0 1.6 %collective-permute-done.3 = f32[19,6,1,128]{3,2,1,0:T(1,128)S(1)} collective-permute-done((f32[19,6,1,128]{3,2,1,0:T(1,128)S(1)}, f32[19,6,1,128]{3,2,1,0:T(1,128)S(1)}, u32[]{:S(2)}, u32[]{:S(2)}) %collective-permute-start.3) | collective-permute-done | bytes 58400 | tf_op jit(solution)/shard_map/ppermute | solution.py:44
  75.6 3.3 %collective-permute-done.2 = f32[19,6,1,128]{3,2,1,0:T(1,128)S(1)} collective-permute-done((f32[19,6,1,128]{3,2,1,0:T(1,128)S(1)}, f32[19,6,1,128]{3,2,1,0:T(1,128)S(1)}, u32[]{:S(2)}, u32[]{:S(2)}) %collective-permute-start.2) | collective-permute-done | bytes 58400 | tf_op jit(solution)/shard_map/ppermute | solution.py:43
  79.4 0.2 bitcast_add_fusion
  79.6 0.1 add_subtract_fusion
  79.7 0.1 add_subtract_fusion.1
  79.8 0.2 fusion.404
  80.0 0.6 fusion.1
  80.6 14.2 %psum.15 = f32[3,512]{1,0:T(4,128)S(1)} all-reduce(f32[3,512]{1,0:T(4,128)S(1)} %fusion.1), channel_id=1, replica_groups=mesh['plate'=4,'sub'=8] {'sub'}, use_global_device_ids=true, to_apply=%region_6.7 | all-reduce | flops 1536 | bytes 12288 | tf_op jit(solution)/shard_map/psum | solution.py:143
  94.8 0.6 fusion.2
  95.4 0.2 fusion.396
  96.5 1.3 %collective-permute-start.5 = (f32[19,1,16,128]{3,2,1,0:T(8,128)S(1)}, f32[19,1,16,128]{3,2,1,0:T(8,128)S(1)}, u32[]{:S(2)}, u32[]{:S(2)}) collective-permute-start(f32[19,1,16,128]{3,2,1,0:T(8,128)S(1)} %get-tuple-element.83), channel_id=1, source_target_pairs={{8,0},{16,8},{24,16},{0,24},{9,1},{17,9},{25,17},{1,25},{10,2},{18... | collective-permute-start | bytes 466952 | tf_op jit(solution)/shard_map/ppermute | solution.py:44
  97.7 0.8 collective-permute-start.4
  98.5 0.6 constant_dynamic-slice_fusion
  99.3 0.7 dynamic-slice_add_fusion
  100.0 3.3 %collective-permute-done.5 = f32[19,1,16,128]{3,2,1,0:T(8,128)S(1)} collective-permute-done((f32[19,1,16,128]{3,2,1,0:T(8,128)S(1)}, f32[19,1,16,128]{3,2,1,0:T(8,128)S(1)}, u32[]{:S(2)}, u32[]{:S(2)}) %collective-permute-start.5) | collective-permute-done | bytes 155680 | tf_op jit(solution)/shard_map/ppermute | solution.py:44
  103.3 1.8 %collective-permute-done.4 = f32[19,1,16,128]{3,2,1,0:T(8,128)S(1)} collective-permute-done((f32[19,1,16,128]{3,2,1,0:T(8,128)S(1)}, f32[19,1,16,128]{3,2,1,0:T(8,128)S(1)}, u32[]{:S(2)}, u32[]{:S(2)}) %collective-permute-start.4) | collective-permute-done | bytes 155680 | tf_op jit(solution)/shard_map/ppermute | solution.py:43
  105.2 0.1 pad_maximum_fusion
  105.3 0.5 collective-permute-start.6
  105.8 5.0 %collective-permute-done.6 = f32[19,6,1,128]{3,2,1,0:T(1,128)S(1)} collective-permute-done((f32[19,6,1,128]{3,2,1,0:T(1,128)S(1)}, f32[19,6,1,128]{3,2,1,0:T(1,128)S(1)}, u32[]{:S(2)}, u32[]{:S(2)}) %collective-permute-start.6) | collective-permute-done | bytes 58400 | tf_op jit(solution)/shard_map/ppermute | solution.py:43
  110.8 0.1 constant_dynamic-update-slice_fusion.51
  111.7 0.1 constant_dynamic-update-slice_fusion.45
  111.8 0.1 constant_dynamic-update-slice_fusion.44
  111.9 0.1 constant_dynamic-update-slice_fusion.43
  111.9 0.1 constant_dynamic-update-slice_fusion.42
  112.0 0.1 constant_dynamic-update-slice_fusion.41
  112.1 0.1 constant_dynamic-update-slice_fusion.40
  112.2 0.1 constant_dynamic-update-slice_fusion.39
  112.3 0.1 constant_dynamic-update-slice_fusion.38
  112.3 0.8 copy-done.1
  (119 shorter events, 3.7 us)
Async XLA Ops:
  0.6 1.9 %copy-start = (f32[19,4,16,128]{3,2,1,0:T(8,128)S(1)}, f32[19,4,16,128]{3,2,1,0:T(8,128)}, u32[]{:S(2)}) copy-start(f32[19,4,16,128]{3,2,1,0:T(8,128)} %param.7) | copy-start | bytes 1867780
  2.6 0.7 copy-start.3
  17.7 0.7 copy-start.4
  31.1 0.7 copy-start.5
  31.1 0.7 copy-start.6
  31.2 0.7 copy-start.7
  62.0 0.8 copy-start.2
  63.5 6.7 %collective-permute-start.1 = (f32[19,1,16,128]{3,2,1,0:T(8,128)S(1)}, f32[19,1,16,128]{3,2,1,0:T(8,128)S(1)}, u32[]{:S(2)}, u32[]{:S(2)}) collective-permute-start(f32[19,1,16,128]{3,2,1,0:T(8,128)S(1)} %get-tuple-element.86), channel_id=1, source_target_pairs={{8,0},{16,8},{24,16},{0,24},{9,1},{17,9},{25,17},{1,25},{10,2},{18... | collective-permute-start | bytes 466952 | tf_op jit(solution)/shard_map/ppermute | solution.py:44
  66.0 7.1 %collective-permute-start = (f32[19,1,16,128]{3,2,1,0:T(8,128)S(1)}, f32[19,1,16,128]{3,2,1,0:T(8,128)S(1)}, u32[]{:S(2)}, u32[]{:S(2)}) collective-permute-start(f32[19,1,16,128]{3,2,1,0:T(8,128)S(1)} %get-tuple-element.87), channel_id=1, source_target_pairs={{0,8},{8,16},{16,24},{24,0},{1,9},{9,17},{17,25},{25,1},{2,10},{10... | collective-permute-start | bytes 466952 | tf_op jit(solution)/shard_map/ppermute | solution.py:43
  73.4 2.2 %collective-permute-start.3 = (f32[19,6,1,128]{3,2,1,0:T(1,128)S(1)}, f32[19,6,1,128]{3,2,1,0:T(1,128)S(1)}, u32[]{:S(2)}, u32[]{:S(2)}) collective-permute-start(f32[19,6,1,128]{3,2,1,0:T(1,128)S(1)} %get-tuple-element.74), channel_id=1, source_target_pairs={{1,0},{2,1},{3,2},{4,3},{5,4},{6,5},{7,6},{0,7},{9,8},{10,9},{11,1... | collective-permute-start | bytes 175112 | tf_op jit(solution)/shard_map/ppermute | solution.py:44
  73.5 5.5 %collective-permute-start.2 = (f32[19,6,1,128]{3,2,1,0:T(1,128)S(1)}, f32[19,6,1,128]{3,2,1,0:T(1,128)S(1)}, u32[]{:S(2)}, u32[]{:S(2)}) collective-permute-start(f32[19,6,1,128]{3,2,1,0:T(1,128)S(1)} %get-tuple-element.75), channel_id=1, source_target_pairs={{0,1},{1,2},{2,3},{3,4},{4,5},{5,6},{6,7},{7,0},{8,9},{9,10},{10,1... | collective-permute-start | bytes 175112 | tf_op jit(solution)/shard_map/ppermute | solution.py:43
  96.5 6.9 %collective-permute-start.5 = (f32[19,1,16,128]{3,2,1,0:T(8,128)S(1)}, f32[19,1,16,128]{3,2,1,0:T(8,128)S(1)}, u32[]{:S(2)}, u32[]{:S(2)}) collective-permute-start(f32[19,1,16,128]{3,2,1,0:T(8,128)S(1)} %get-tuple-element.83), channel_id=1, source_target_pairs={{8,0},{16,8},{24,16},{0,24},{9,1},{17,9},{25,17},{1,25},{10,2},{18... | collective-permute-start | bytes 466952 | tf_op jit(solution)/shard_map/ppermute | solution.py:44
  97.7 7.4 %collective-permute-start.4 = (f32[19,1,16,128]{3,2,1,0:T(8,128)S(1)}, f32[19,1,16,128]{3,2,1,0:T(8,128)S(1)}, u32[]{:S(2)}, u32[]{:S(2)}) collective-permute-start(f32[19,1,16,128]{3,2,1,0:T(8,128)S(1)} %get-tuple-element.84), channel_id=1, source_target_pairs={{0,8},{8,16},{16,24},{24,0},{1,9},{9,17},{17,25},{25,1},{2,10},{10... | collective-permute-start | bytes 466952 | tf_op jit(solution)/shard_map/ppermute | solution.py:43
  105.3 5.5 %collective-permute-start.7 = (f32[19,6,1,128]{3,2,1,0:T(1,128)S(1)}, f32[19,6,1,128]{3,2,1,0:T(1,128)S(1)}, u32[]{:S(2)}, u32[]{:S(2)}) collective-permute-start(f32[19,6,1,128]{3,2,1,0:T(1,128)S(1)} %get-tuple-element.70), channel_id=1, source_target_pairs={{1,0},{2,1},{3,2},{4,3},{5,4},{6,5},{7,6},{0,7},{9,8},{10,9},{11,1... | collective-permute-start | bytes 175112 | tf_op jit(solution)/shard_map/ppermute | solution.py:44
  105.3 5.5 %collective-permute-start.6 = (f32[19,6,1,128]{3,2,1,0:T(1,128)S(1)}, f32[19,6,1,128]{3,2,1,0:T(1,128)S(1)}, u32[]{:S(2)}, u32[]{:S(2)}) collective-permute-start(f32[19,6,1,128]{3,2,1,0:T(1,128)S(1)} %get-tuple-element.71), channel_id=1, source_target_pairs={{0,1},{1,2},{2,3},{3,4},{4,5},{5,6},{6,7},{7,0},{8,9},{9,10},{10,1... | collective-permute-start | bytes 175112 | tf_op jit(solution)/shard_map/ppermute | solution.py:43
  112.3 0.8 copy-start.1
where the time goes:
time: 114 us; the launch traced here: 113 us
  blocking collectives  69.9 us (61%)
  waiting for transfers between devices  22 us (19%)
  local copies, waits for them, and re-layouts  6.08 us (5%)
  other arithmetic  5.92 us (5%)
  starting transfers between devices  5.7 us (5%)
  matrix products  2.36 us (2%)
  between operations  1.23 us (1%)
    psum x2, blocking collectives, shards(): marker_vel = lax.psum(partial_value, 'sub')  28.8 us
    all_gather x1, blocking collectives, shards(): corners = lax.all_gather(marker_corner, 'sub', axis=1, tiled=True)  14.4 us
    all_gather x1, blocking collectives, shards(): state = lax.all_gather(stacked, 'sub', axis=1, tiled=True)  14 us
    ppermute x4, waiting for transfers between devices, extended(): before = lax.ppermute(last, axis, up)  13 us
    all_gather x1, blocking collectives, shards(): fracs = lax.all_gather(marker_frac, 'sub', axis=1, tiled=True)  12.7 us
    ppermute x4, waiting for transfers between devices, extended(): after = lax.ppermute(initial, axis, down)  9.02 us
    ppermute x4, starting transfers between devices, extended(): after = lax.ppermute(initial, axis, down)  3.88 us
    unnamed x21, local copies, waits for them, and re-layouts  3.79 us
  transfers between devices with their start and end apart: 8, of which 7 were waited for; matrix products, arithmetic and copies ran while one was open for 1% of the time, Pallas kernels for 0%

commit v1 on v0

v1 whole, which is shorter than its diff:
```python
import functools

import jax
import jax.numpy as jnp
from jax import lax
from jax.experimental import pallas as pl
from jax.experimental.pallas import tpu as pltpu
from jax.sharding import PartitionSpec as P

STEPS = 2
DIRS = [
    (0, 0, 0),
    (1, 0, 0),
    (-1, 0, 0),
    (0, 1, 0),
    (0, -1, 0),
    (0, 0, 1),
    (0, 0, -1),
    (1, 1, 0),
    (-1, -1, 0),
    (1, -1, 0),
    (-1, 1, 0),
    (1, 0, 1),
    (-1, 0, -1),
    (1, 0, -1),
    (-1, 0, 1),
    (0, 1, 1),
    (0, -1, -1),
    (0, 1, -1),
    (0, -1, 1),
]
WEIGHTS = [1.0 / 3.0] + [1.0 / 18.0] * 6 + [1.0 / 36.0] * 12
PAIRS = [(i, i + 1) for i in range(1, 19, 2)]
KAPPA = 4.0
RELAX = 0.9
MESH = pl.DeviceIdType.MESH

X_UP = [i for i in range(19) if DIRS[i][0] == 1]
X_DN = [i for i in range(19) if DIRS[i][0] == -1]
Y_UP = [i for i in range(19) if DIRS[i][1] == 1]
Y_DN = [i for i in range(19) if DIRS[i][1] == -1]
EDGES = [i for i in range(19) if DIRS[i][0] and DIRS[i][1]]
ORDER = X_UP + X_DN + [i for i in range(19) if DIRS[i][0] == 0]
SLOT = [ORDER.index(i) for i in range(19)]


def signed_sum(index, vectors):
    total = None
    for axis in range(3):
        sign = DIRS[index][axis]
        if sign == 0:
            continue
        if total is None:
            total = vectors[axis] if sign == 1 else -vectors[axis]
        else:
            total = total + vectors[axis] if sign == 1 else total - vectors[axis]
    return total


def kernel_weights(frac):
    root = jnp.sqrt(1.0 + 4.0 * frac - 4.0 * frac * frac)
    second = (3.0 - 2.0 * frac + root) / 8.0
    third = (1.0 + 2.0 * frac + root) / 8.0
    return (0.5 - third, second, third, 0.5 - second)


def dense_rows(first, weights, length):
    cells = lax.broadcasted_iota(jnp.int32, (length, first.shape[1]), 0)
    offset = cells - first
    result = jnp.zeros(offset.shape, jnp.float32)
    for k in range(4):
        result = jnp.where(offset == k, weights[k], result)
    return result


def split(x):
    high = x.astype(jnp.bfloat16)
    return high, (x - high.astype(jnp.float32)).astype(jnp.bfloat16)


def dot3(a, b, dims):
    dot = functools.partial(
        lax.dot_general, dimension_numbers=(dims, ((), ())), preferred_element_type=jnp.float32
    )
    return dot(a[0], b[0]) + dot(a[1], b[0]) + dot(a[0], b[1])


def body(
    n_plate,
    n_sub,
    pops_ref,
    solid_ref,
    corner_ref,
    frac_ref,
    target_ref,
    stiff_ref,
    disp_ref,
    out_ref,
    disp_out,
    force_out,
    marks,
    velsum,
    post,
    mid,
    x_recv,
    y_send,
    y_recv,
    e_send,
    e_recv,
    own,
    mark_s,
    mark_r,
    vel_s,
    vel_r,
    halo_s,
    halo_r,
):
    _, nx, ny, nz = pops_ref.shape
    count = frac_ref.shape[1]
    lanes = 2 * count
    plate, me = lax.axis_index("plate"), lax.axis_index("sub")

    def at(d_plate, d_sub):
        return (lax.rem(plate + d_plate + n_plate, n_plate), lax.rem(me + d_sub + n_sub, n_sub))

    targets = [(1, 0), (-1, 0), (0, 1), (0, -1)] + [DIRS[i][:2] for i in EDGES]
    greeted = {(0, k) for k in range(1, n_sub)}
    greeted |= {(a % n_plate, b % n_sub) for a, b in targets}
    greeted = sorted(greeted)
    barrier = pltpu.get_barrier_semaphore()
    for a, b in greeted:
        pl.semaphore_signal(barrier, inc=1, device_id=at(a, b), device_id_type=MESH)

    right_half = jnp.zeros((8, lanes), jnp.float32)
    own[...] = right_half
    own[0:3, 0:count] = corner_ref[...].astype(jnp.float32)
    own[3:6, 0:count] = disp_ref[...]
    right_half = pltpu.roll(own[...], count, 1)
    own[0:3, 0:count] = frac_ref[...]
    own[3:6, 0:count] = target_ref[...]
    own[6:7, 0:count] = stiff_ref[...]
    left = lax.broadcasted_iota(jnp.int32, (8, lanes), 1) < count
    marks[me] = jnp.where(left, own[...], right_half)

    pl.semaphore_wait(barrier, len(greeted))

    def to_all(buffer, send, recv):
        copies = []
        for k in range(1, n_sub):
            copy = pltpu.make_async_remote_copy(
                src_ref=buffer.at[me],
                dst_ref=buffer.at[me],
                send_sem=send.at[k],
                recv_sem=recv.at[k],
                device_id=at(0, k),
                device_id_type=MESH,
            )
            copy.start()
            copies.append(copy)
        return copies

    def all_here(buffer, send, recv):
        for k in range(1, n_sub):
            slot = lax.rem(me - k + n_sub, n_sub)
            pltpu.make_async_remote_copy(
                src_ref=buffer.at[slot],
                dst_ref=buffer.at[slot],
                send_sem=send.at[k],
                recv_sem=recv.at[k],
                device_id=at(0, k),
                device_id_type=MESH,
            ).wait_recv()

    sent = to_all(marks, mark_s, mark_r)

    def moments(pops):
        density = pops[0]
        for i in range(1, 19):
            density = density + pops[i]
        comps = []
        for axis in range(3):
            total = jnp.zeros_like(density)
            for i in range(19):
                if DIRS[i][axis] == 1:
                    total = total + pops[i]
                elif DIRS[i][axis] == -1:
                    total = total - pops[i]
            comps.append(total)
        inverse = 1.0 / density
        return density, [c * inverse for c in comps]

    fluid = solid_ref[...] == 0
    keep = 1.0 - 1.0 / RELAX
    row = lax.broadcasted_iota(jnp.int32, (nx, ny, nz), 1)
    disp = None
    for step in range(STEPS):
        source = pops_ref if step == 0 else mid
        density, velocity = moments([source[i] for i in range(19)])
        flat = split(jnp.concatenate(velocity, 0).reshape(3 * nx * ny, nz))
        if step == 0:
            all_here(marks, mark_s, mark_r)
            firsts, seconds = [], []
            for pair in range(n_sub // 2):
                a, b = marks[2 * pair], marks[2 * pair + 1]
                firsts.append(jnp.where(left, a, pltpu.roll(b, count, 1)))
                seconds.append(jnp.where(left, pltpu.roll(a, count, 1), b))
            first, second = jnp.concatenate(firsts, 1), jnp.concatenate(seconds, 1)
            total = first.shape[1]
            corners = second[0:3].astype(jnp.int32)
            x_first = corners[0:1] - plate * nx
            y_first = corners[1:2] - me * ny
            x_w, y_w, z_w = [kernel_weights(first[k : k + 1]) for k in range(3)]
            y_rows = dense_rows(y_first, y_w, ny)
            planes = []
            for x in range(nx):
                w = jnp.zeros_like(x_w[0])
                for k in range(4):
                    w = jnp.where(x_first == x - k, x_w[k], w)
                planes.append(w * y_rows)
            xy_rows = jnp.concatenate(planes, 0)
            z_rows = split(dense_rows(corners[2:3], z_w, nz))
            target = [first[3 + k : 4 + k] for k in range(3)]
            spring = first[6:7]
            disp = [second[3 + k : 4 + k] for k in range(3)]
        along = dot3(flat, z_rows, ((1,), (0,)))
        cells = nx * ny
        partial = [
            jnp.sum(along[k * cells : (k + 1) * cells] * xy_rows, 0, keepdims=True)
            for k in range(3)
        ]
        velsum[step, me] = jnp.concatenate(partial, 1)
        sent += to_all(velsum.at[step], vel_s.at[step], vel_r.at[step])

        speed = velocity[0] * velocity[0] + velocity[1] * velocity[1] + velocity[2] * velocity[2]
        scaled = density * (1.0 / RELAX)
        base = scaled * (1.0 - 1.5 * speed)
        rest = source[0]
        post[step, SLOT[0]] = jnp.where(fluid, keep * rest + WEIGHTS[0] * base, rest)
        for i, j in PAIRS:
            proj = signed_sum(i, velocity)
            flow = scaled * proj
            even = WEIGHTS[i] * (base + 4.5 * flow * proj)
            odd = (3.0 * WEIGHTS[i]) * flow
            a, b = source[i], source[j]
            post[step, SLOT[i]] = jnp.where(fluid, keep * a + (even + odd), b)
            post[step, SLOT[j]] = jnp.where(fluid, keep * b + (even - odd), a)

        all_here(velsum.at[step], vel_s.at[step], vel_r.at[step])
        summed = velsum[step, 0]
        for s in range(1, n_sub):
            summed = summed + velsum[step, s]
        moved = [summed[:, k * total : (k + 1) * total] for k in range(3)]
        force = [KAPPA * (target[k] - moved[k]) - spring * disp[k] for k in range(3)]
        disp = [disp[k] + moved[k] for k in range(3)]
        weighted = split(jnp.concatenate([xy_rows * force[k] for k in range(3)], 0))
        spread = dot3(weighted, z_rows, ((1,), (1,))).reshape(3, nx, ny, nz)
        spread = [jnp.where(fluid, spread[k], 0.0) for k in range(3)]
        for i, j in PAIRS:
            push = (3.0 * WEIGHTS[i]) * signed_sum(i, spread)
            post[step, SLOT[i]] = post[step, SLOT[i]] + push
            post[step, SLOT[j]] = post[step, SLOT[j]] - push

        for n, i in enumerate(Y_UP):
            y_send[step, 0, n] = post[step, SLOT[i], :, ny - 1 : ny, :]
        for n, i in enumerate(Y_DN):
            y_send[step, 1, n] = post[step, SLOT[i], :, 0:1, :]
        for n, i in enumerate(EDGES):
            x = nx - 1 if DIRS[i][0] == 1 else 0
            y = ny - 1 if DIRS[i][1] == 1 else 0
            e_send[step, n] = post[step, SLOT[i], x, y : y + 1, :]
        ends = [
            (post.at[step, pl.ds(0, len(X_UP)), nx - 1], x_recv.at[step, 0]),
            (post.at[step, pl.ds(len(X_UP), len(X_DN)), 0], x_recv.at[step, 1]),
            (y_send.at[step, 0], y_recv.at[step, 0]),
            (y_send.at[step, 1], y_recv.at[step, 1]),
        ] + [(e_send.at[step, n], e_recv.at[step, n]) for n in range(len(EDGES))]
        halo = []
        for n, ((src, dst), (a, b)) in enumerate(zip(ends, targets)):
            copy = pltpu.make_async_remote_copy(
                src_ref=src,
                dst_ref=dst,
                send_sem=halo_s.at[step, n],
                recv_sem=halo_r.at[step, n],
                device_id=at(a, b),
                device_id_type=MESH,
            )
            copy.start()
            halo.append(copy)
        sent += halo

        dest = mid if step < STEPS - 1 else out_ref
        inner = [i for i in range(19) if not (DIRS[i][0] or DIRS[i][1])]
        for i in inner + [i for i in range(19) if i not in inner]:
            if i == 1:
                for copy in halo:
                    copy.wait_recv()
            dx, dy, dz = DIRS[i]
            cells_i = post[step, SLOT[i]]
            if dx == 1:
                cells_i = jnp.concatenate(
                    [x_recv[step, 0, X_UP.index(i)][None], cells_i[: nx - 1]], 0
                )
            elif dx == -1:
                cells_i = jnp.concatenate([cells_i[1:], x_recv[step, 1, X_DN.index(i)][None]], 0)
            if dy:
                side, names = (0, Y_UP) if dy == 1 else (1, Y_DN)
                edge = y_recv[step, side, names.index(i)]
                if dx == 1:
                    edge = jnp.concatenate(
                        [e_recv[step, EDGES.index(i)][None], edge[: nx - 1]], 0
                    )
                elif dx == -1:
                    edge = jnp.concatenate([edge[1:], e_recv[step, EDGES.index(i)][None]], 0)
                turned = pltpu.roll(cells_i, dy % ny, 1)
                cells_i = jnp.where(row == (0 if dy == 1 else ny - 1), edge, turned)
            if dz:
                cells_i = pltpu.roll(cells_i, dz % nz, 2)
            dest[i] = cells_i

    for values, result in ((disp, disp_out), (force, force_out)):
        for k in range(3):
            mine = jnp.zeros((1, lanes), jnp.float32)
            for pair in range(n_sub // 2):
                part = values[k][:, pair * lanes : (pair + 1) * lanes]
                mine = jnp.where(me // 2 == pair, part, mine)
            mine = jnp.where(lax.rem(me, 2) == 0, mine, pltpu.roll(mine, count, 1))
            result[k : k + 1, :] = mine[:, :count]
    for copy in sent:
        copy.wait_send()


def shards(n_plate, n_sub, populations, solid, corner, frac, target, stiffness, displacement):
    _, nx, ny, nz = populations.shape
    count = stiffness.shape[0]
    f32 = jnp.float32
    vmem = pl.BlockSpec(memory_space=pltpu.VMEM)
    total = count * n_sub
    faces = len(X_UP)
    return pl.pallas_call(
        functools.partial(body, n_plate, n_sub),
        out_shape=(
            jax.ShapeDtypeStruct(populations.shape, f32),
            jax.ShapeDtypeStruct(displacement.shape, f32),
            jax.ShapeDtypeStruct(displacement.shape, f32),
        ),
        in_specs=[vmem] * 7,
        out_specs=(vmem,) * 3,
        scratch_shapes=[
            pltpu.VMEM((n_sub, 8, 2 * count), f32),
            pltpu.VMEM((STEPS, n_sub, 1, 3 * total), f32),
            pltpu.VMEM((STEPS, 19, nx, ny, nz), f32),
            pltpu.VMEM((19, nx, ny, nz), f32),
            pltpu.VMEM((STEPS, 2, faces, ny, nz), f32),
            pltpu.VMEM((STEPS, 2, faces, nx, 1, nz), f32),
            pltpu.VMEM((STEPS, 2, faces, nx, 1, nz), f32),
            pltpu.VMEM((STEPS, len(EDGES), 1, nz), f32),
            pltpu.VMEM((STEPS, len(EDGES), 1, nz), f32),
            pltpu.VMEM((8, 2 * count), f32),
            pltpu.SemaphoreType.DMA((n_sub,)),
            pltpu.SemaphoreType.DMA((n_sub,)),
            pltpu.SemaphoreType.DMA((STEPS, n_sub)),
            pltpu.SemaphoreType.DMA((STEPS, n_sub)),
            pltpu.SemaphoreType.DMA((STEPS, 8)),
            pltpu.SemaphoreType.DMA((STEPS, 8)),
        ],
        compiler_params=pltpu.CompilerParams(
            collective_id=0, has_side_effects=True, vmem_limit_bytes=40 * 1024 * 1024
        ),
    )(populations, solid, corner, frac, target, stiffness[None], displacement)


def solution(mesh):
    in_specs = (
        P(None, "plate", "sub", None),
        P("plate", "sub", None),
        P(None, ("plate", "sub")),
        P(None, ("plate", "sub")),
        P(None, ("plate", "sub")),
        P(("plate", "sub")),
        P(None, ("plate", "sub")),
    )
    out_specs = (
        P(None, "plate", "sub", None),
        P(None, ("plate", "sub")),
        P(None, ("plate", "sub")),
    )
    run = functools.partial(shards, mesh.shape["plate"], mesh.shape["sub"])
    return jax.shard_map(run, mesh=mesh, in_specs=in_specs, out_specs=out_specs, check_vma=False)
```

time: 114 us -> 36.7 us (0.32)
  blocking collectives: 69.9 us -> 0 us
  Pallas kernels: 0 us -> 28.5 us
  waiting for transfers between devices: 22 us -> 0 us
  other arithmetic: 5.92 us -> 0 us
  starting transfers between devices: 5.7 us -> 0 us
  matrix products: 2.36 us -> 0 us
    all_gather x3 -> x0, blocking collectives: 41.1 us -> none  [the longest x1 14.4 us: shards(): corners = lax.all_gather(marker_corner, 'sub', axis=1, tiled=True)]
    psum x2 -> x0, blocking collectives: 28.8 us -> none  [shards(): marker_vel = lax.psum(partial_value, 'sub')]
    pallas_call x0 -> x1, Pallas kernels: none -> 28.5 us  [shards(): pl.pallas_call(functools.partial(body, n_plate, n_sub), out_shape=(jax.Sh...]
    ppermute x8 -> x0, waiting for transfers between devices: 22 us -> none  [the longest x4 13 us: extended(): before = lax.ppermute(last, axis, up)]
    ppermute x8 -> x0, starting transfers between devices: 5.7 us -> none  [the longest x4 3.88 us: extended(): after = lax.ppermute(initial, axis, down)]
    unnamed x21 -> x17, local copies, waits for them, and re-layouts: 3.79 us -> 7.19 us
    dot_general x4 -> x0, matrix products: 2.36 us -> none  [the longest x2 1.22 us: shards(): jnp.einsum('kcz,zm->kcm', flat, z_rows, precision=lax.Precision.HIGHEST)]
    sub x8 -> x0, other arithmetic: 2.21 us -> none  [the longest x4 2.14 us: moments(): total = total - pops[index]]
  transfers between devices with their start and end apart: 8 -> 0, of which waited for: 7 -> 0; matrix products, arithmetic and copies ran while one was open for 1% -> 0% of each run, Pallas kernels for 0% -> 0%
where the time goes in v1:
time: 36.7 us; the launch traced here: 36.4 us
  Pallas kernels  28.5 us (78%)
  local copies, waits for them, and re-layouts  7.19 us (20%)
  between operations  0.66 us (2%)
    pallas_call x1, Pallas kernels, shards(): pl.pallas_call(functools.partial(body, n_plate, n_sub), out_shape=(jax.Sh...  28.5 us
    unnamed x17, local copies, waits for them, and re-layouts  7.19 us

profile of v1, /device:TPU:0, one launch (start us, length us, event | category | flops | bytes accessed | tf_op | source)
XLA Modules:
  0.0 36.4 jit_solution(9165367804520346054)
XLA Ops:
  0.6 0.0 copy-start.6
  0.6 0.6 %copy-done.6 = f32[64]{0:T(128)S(1)} copy-done((f32[64]{0:T(128)S(1)}, f32[64]{0:T(128)}, u32[]{:S(2)}) %copy-start.6) | copy-done | bytes 280
  1.3 0.0 copy-start
  1.3 1.1 %copy-done = f32[19,4,16,128]{3,2,1,0:T(8,128)S(1)} copy-done((f32[19,4,16,128]{3,2,1,0:T(8,128)S(1)}, f32[19,4,16,128]{3,2,1,0:T(8,128)}, u32[]{:S(2)}) %copy-start) | copy-done | bytes 622616
  2.4 0.0 copy-start.1
  2.4 0.8 %copy-done.1 = s32[4,16,128]{2,1,0:T(8,128)S(1)} copy-done((s32[4,16,128]{2,1,0:T(8,128)S(1)}, s32[4,16,128]{2,1,0:T(8,128)}, u32[]{:S(2)}) %copy-start.1) | copy-done | bytes 32792
  3.1 0.0 copy-start.2
  3.1 0.7 %copy-done.2 = s32[3,64]{1,0:T(4,128)S(1)} copy-done((s32[3,64]{1,0:T(4,128)S(1)}, s32[3,64]{1,0:T(4,128)}, u32[]{:S(2)}) %copy-start.2) | copy-done | bytes 792
  3.8 0.0 copy-start.3
  3.8 0.7 %copy-done.3 = f32[3,64]{1,0:T(4,128)S(1)} copy-done((f32[3,64]{1,0:T(4,128)S(1)}, f32[3,64]{1,0:T(4,128)}, u32[]{:S(2)}) %copy-start.3) | copy-done | bytes 792
  4.5 0.0 copy-start.4
  4.5 0.7 %copy-done.4 = f32[3,64]{1,0:T(4,128)S(1)} copy-done((f32[3,64]{1,0:T(4,128)S(1)}, f32[3,64]{1,0:T(4,128)}, u32[]{:S(2)}) %copy-start.4) | copy-done | bytes 792
  5.2 0.0 copy-start.5
  5.2 0.7 %copy-done.5 = f32[3,64]{1,0:T(4,128)S(1)} copy-done((f32[3,64]{1,0:T(4,128)S(1)}, f32[3,64]{1,0:T(4,128)}, u32[]{:S(2)}) %copy-start.5) | copy-done | bytes 792
  5.9 28.5 %shard_map.94 = (f32[19,4,16,128]{3,2,1,0:T(8,128)S(1)}, f32[3,64]{1,0:T(4,128)S(1)}, f32[3,64]{1,0:T(4,128)S(1)}) custom-call(f32[19,4,16,128]{3,2,1,0:T(8,128)S(1)} %copy-done, s32[4,16,128]{2,1,0:T(8,128)S(1)} %copy-done.1, s32[3,64]{1,0:T(4,128)S(1)} %copy-done.2, f32[3,64]{1,0:T(4,128)S(1)} %copy-done.3, f32[3,64]{1,0:T(4,128)S(1)} %copy-done.4, ...), custom_call_target="tpu_custom_call" | custom-call | tf_op jit(solution)/shard_map/pallas_call | solution.py:339
  34.4 0.8 %copy.13 = f32[19,4,16,128]{3,2,1,0:T(8,128)} copy(f32[19,4,16,128]{3,2,1,0:T(8,128)S(1)} %get-tuple-element.6) | data formatting | bytes 1245184
  35.2 0.6 %copy.14 = f32[3,64]{1,0:T(4,128)} copy(f32[3,64]{1,0:T(4,128)S(1)} %get-tuple-element.7) | data formatting | bytes 1536
  35.8 0.6 %copy.15 = f32[3,64]{1,0:T(4,128)} copy(f32[3,64]{1,0:T(4,128)S(1)} %get-tuple-element.8) | data formatting | bytes 1536
Async XLA Ops:
  0.6 0.7 %copy-start.6 = (f32[64]{0:T(128)S(1)}, f32[64]{0:T(128)}, u32[]{:S(2)}) copy-start(f32[64]{0:T(128)} %param.12) | copy-start | bytes 772
  1.3 1.1 %copy-start = (f32[19,4,16,128]{3,2,1,0:T(8,128)S(1)}, f32[19,4,16,128]{3,2,1,0:T(8,128)}, u32[]{:S(2)}) copy-start(f32[19,4,16,128]{3,2,1,0:T(8,128)} %pops_ref.1) | copy-start | bytes 1867780
  2.4 0.8 %copy-start.1 = (s32[4,16,128]{2,1,0:T(8,128)S(1)}, s32[4,16,128]{2,1,0:T(8,128)}, u32[]{:S(2)}) copy-start(s32[4,16,128]{2,1,0:T(8,128)} %solid_ref.1) | copy-start | bytes 98308
  3.1 0.7 %copy-start.2 = (s32[3,64]{1,0:T(4,128)S(1)}, s32[3,64]{1,0:T(4,128)}, u32[]{:S(2)}) copy-start(s32[3,64]{1,0:T(4,128)} %corner_ref.1) | copy-start | bytes 2308
  3.8 0.7 %copy-start.3 = (f32[3,64]{1,0:T(4,128)S(1)}, f32[3,64]{1,0:T(4,128)}, u32[]{:S(2)}) copy-start(f32[3,64]{1,0:T(4,128)} %frac_ref.1) | copy-start | bytes 2308
  4.5 0.7 %copy-start.4 = (f32[3,64]{1,0:T(4,128)S(1)}, f32[3,64]{1,0:T(4,128)}, u32[]{:S(2)}) copy-start(f32[3,64]{1,0:T(4,128)} %target_ref.1) | copy-start | bytes 2308
  5.2 0.7 %copy-start.5 = (f32[3,64]{1,0:T(4,128)S(1)}, f32[3,64]{1,0:T(4,128)}, u32[]{:S(2)}) copy-start(f32[3,64]{1,0:T(4,128)} %disp_ref.1) | copy-start | bytes 2308

commit v2 on v1

--- a/solution.py
+++ b/solution.py
@@ -88,6 +88,16 @@
 def body(
     n_plate,
     n_sub,
+    pops_hbm,
+    solid_hbm,
+    corner_hbm,
+    frac_hbm,
+    target_hbm,
+    stiff_hbm,
+    disp_hbm,
+    out_ref,
+    disp_out,
+    force_out,
     pops_ref,
     solid_ref,
     corner_ref,
@@ -95,9 +105,6 @@
     target_ref,
     stiff_ref,
     disp_ref,
-    out_ref,
-    disp_out,
-    force_out,
     marks,
     velsum,
     post,
@@ -114,6 +121,7 @@
     vel_r,
     halo_s,
     halo_r,
+    local,
 ):
     _, nx, ny, nz = pops_ref.shape
     count = frac_ref.shape[1]
@@ -130,6 +138,25 @@
     barrier = pltpu.get_barrier_semaphore()
     for a, b in greeted:
         pl.semaphore_signal(barrier, inc=1, device_id=at(a, b), device_id_type=MESH)
+
+    loads = [
+        pltpu.make_async_copy(src, dst, local.at[n])
+        for n, (src, dst) in enumerate(
+            (
+                (corner_hbm, corner_ref),
+                (disp_hbm, disp_ref),
+                (frac_hbm, frac_ref),
+                (target_hbm, target_ref),
+                (stiff_hbm, stiff_ref),
+                (pops_hbm, pops_ref),
+                (solid_hbm, solid_ref),
+            )
+        )
+    ]
+    for load in loads:
+        load.start()
+    for load in loads[:5]:
+        load.wait()
 
     right_half = jnp.zeros((8, lanes), jnp.float32)
     own[...] = right_half
@@ -189,6 +216,8 @@
         inverse = 1.0 / density
         return density, [c * inverse for c in comps]
 
+    for load in loads[5:]:
+        load.wait()
     fluid = solid_ref[...] == 0
     keep = 1.0 - 1.0 / RELAX
     row = lax.broadcasted_iota(jnp.int32, (nx, ny, nz), 1)
@@ -289,19 +318,26 @@
         sent += halo
 
         dest = mid if step < STEPS - 1 else out_ref
-        inner = [i for i in range(19) if not (DIRS[i][0] or DIRS[i][1])]
-        for i in inner + [i for i in range(19) if i not in inner]:
-            if i == 1:
-                for copy in halo:
-                    copy.wait_recv()
-            dx, dy, dz = DIRS[i]
+        for i, (dx, dy, dz) in enumerate(DIRS):
             cells_i = post[step, SLOT[i]]
-            if dx == 1:
-                cells_i = jnp.concatenate(
-                    [x_recv[step, 0, X_UP.index(i)][None], cells_i[: nx - 1]], 0
-                )
-            elif dx == -1:
-                cells_i = jnp.concatenate([cells_i[1:], x_recv[step, 1, X_DN.index(i)][None]], 0)
+            if dx:
+                cells_i = cells_i[: nx - 1] if dx == 1 else cells_i[1:]
+            if dy:
+                cells_i = pltpu.roll(cells_i, dy % ny, 1)
+            if dz:
+                cells_i = pltpu.roll(cells_i, dz % nz, 2)
+            dest[i, pl.ds(max(dx, 0), nx - abs(dx))] = cells_i
+        for copy in halo:
+            copy.wait_recv()
+        for i, (dx, dy, dz) in enumerate(DIRS):
+            if dx:
+                side, names = (0, X_UP) if dx == 1 else (1, X_DN)
+                face = x_recv[step, side, names.index(i)]
+                if dy:
+                    face = pltpu.roll(face, dy % ny, 0)
+                if dz:
+                    face = pltpu.roll(face, dz % nz, 1)
+                dest[i, 0 if dx == 1 else nx - 1] = face
             if dy:
                 side, names = (0, Y_UP) if dy == 1 else (1, Y_DN)
                 edge = y_recv[step, side, names.index(i)]
@@ -311,11 +347,10 @@
                     )
                 elif dx == -1:
                     edge = jnp.concatenate([edge[1:], e_recv[step, EDGES.index(i)][None]], 0)
-                turned = pltpu.roll(cells_i, dy % ny, 1)
-                cells_i = jnp.where(row == (0 if dy == 1 else ny - 1), edge, turned)
-            if dz:
-                cells_i = pltpu.roll(cells_i, dz % nz, 2)
-            dest[i] = cells_i
+                if dz:
+                    edge = pltpu.roll(edge.reshape(nx, nz), dz % nz, 1).reshape(nx, 1, nz)
+                y = 0 if dy == 1 else ny - 1
+                dest[i, :, y : y + 1, :] = edge
 
     for values, result in ((disp, disp_out), (force, force_out)):
         for k in range(3):
@@ -343,9 +378,16 @@
             jax.ShapeDtypeStruct(displacement.shape, f32),
             jax.ShapeDtypeStruct(displacement.shape, f32),
         ),
-        in_specs=[vmem] * 7,
+        in_specs=[pl.BlockSpec(memory_space=pltpu.HBM)] * 7,
         out_specs=(vmem,) * 3,
         scratch_shapes=[
+            pltpu.VMEM(populations.shape, f32),
+            pltpu.VMEM(solid.shape, jnp.int32),
+            pltpu.VMEM(corner.shape, jnp.int32),
+            pltpu.VMEM(frac.shape, f32),
+            pltpu.VMEM(target.shape, f32),
+            pltpu.VMEM((1, count), f32),
+            pltpu.VMEM(displacement.shape, f32),
             pltpu.VMEM((n_sub, 8, 2 * count), f32),
             pltpu.VMEM((STEPS, n_sub, 1, 3 * total), f32),
             pltpu.VMEM((STEPS, 19, nx, ny, nz), f32),
@@ -362,9 +404,10 @@
             pltpu.SemaphoreType.DMA((STEPS, n_sub)),
             pltpu.SemaphoreType.DMA((STEPS, 8)),
             pltpu.SemaphoreType.DMA((STEPS, 8)),
+            pltpu.SemaphoreType.DMA((7,)),
         ],
         compiler_params=pltpu.CompilerParams(
-            collective_id=0, has_side_effects=True, vmem_limit_bytes=40 * 1024 * 1024
+            collective_id=0, has_side_effects=True, vmem_limit_bytes=62 * 1024 * 1024
         ),
     )(populations, solid, corner, frac, target, stiffness[None], displacement)
 

time: 36.7 us -> 33.4 us (0.910)
  local copies, waits for them, and re-layouts: 7.19 us -> 3.19 us
  Pallas kernels: 28.5 us -> 29.4 us
    unnamed x17 -> x7, local copies, waits for them, and re-layouts: 7.19 us -> 3.19 us
    pallas_call x1, Pallas kernels: 28.5 us -> 29.4 us  [shards(): pl.pallas_call(functools.partial(body, n_plate, n_sub), out_shape=(jax.Sh...]
where the time goes in v2:
time: 33.4 us; the launch traced here: 33.2 us
  Pallas kernels  29.4 us (88%)
  local copies, waits for them, and re-layouts  3.19 us (10%)
  between operations  0.65 us (2%)
    pallas_call x1, Pallas kernels, shards(): pl.pallas_call(functools.partial(body, n_plate, n_sub), out_shape=(jax.Sh...  29.4 us
    unnamed x7, local copies, waits for them, and re-layouts  3.19 us

profile of v2, /device:TPU:0, one launch (start us, length us, event | category | flops | bytes accessed | tf_op | source)
XLA Modules:
  0.0 33.2 jit_solution(15211420951811259247)
XLA Ops:
  0.6 29.4 %shard_map.94 = (f32[19,4,16,128]{3,2,1,0:T(8,128)}, f32[3,64]{1,0:T(4,128)}, f32[3,64]{1,0:T(4,128)}) custom-call(f32[19,4,16,128]{3,2,1,0:T(8,128)} %pops_hbm.1, s32[4,16,128]{2,1,0:T(8,128)} %solid_hbm.1, s32[3,64]{1,0:T(4,128)} %corner_hbm.1, f32[3,64]{1,0:T(4,128)} %frac_hbm.1, f32[3,64]{1,0:T(4,128)} %target_hbm.1, f32[1,64]{1,0:T(1,128)} %bitcast.1, ...), custom_call_target="tpu_custom_call" | custom-call | tf_op jit(solution)/shard_map/pallas_call | solution.py:374
  30.0 0.0 copy-start.1
  30.0 2.0 %copy.13 = f32[19,4,16,128]{3,2,1,0:T(8,128)} copy(f32[19,4,16,128]{3,2,1,0:T(8,128)} %get-tuple-element.6) | data formatting | bytes 1245184
  32.0 0.0 copy-done.1
  32.0 0.0 copy-start
  32.0 0.6 %copy.14 = f32[3,64]{1,0:T(4,128)} copy(f32[3,64]{1,0:T(4,128)S(1)} %copy-done.1) | data formatting | bytes 1536
  32.6 0.1 copy-done
  32.7 0.6 %copy.15 = f32[3,64]{1,0:T(4,128)} copy(f32[3,64]{1,0:T(4,128)S(1)} %copy-done) | data formatting | bytes 1536
Async XLA Ops:
  30.0 2.0 %copy-start.1 = (f32[3,64]{1,0:T(4,128)S(1)}, f32[3,64]{1,0:T(4,128)}, u32[]{:S(2)}) copy-start(f32[3,64]{1,0:T(4,128)} %get-tuple-element.7) | copy-start | bytes 2308
  32.0 0.7 %copy-start = (f32[3,64]{1,0:T(4,128)S(1)}, f32[3,64]{1,0:T(4,128)}, u32[]{:S(2)}) copy-start(f32[3,64]{1,0:T(4,128)} %get-tuple-element.8) | copy-start | bytes 2308

commit v3 on v2

--- a/solution.py
+++ b/solution.py
@@ -33,6 +33,7 @@
 PAIRS = [(i, i + 1) for i in range(1, 19, 2)]
 KAPPA = 4.0
 RELAX = 0.9
+PIECES = 4
 MESH = pl.DeviceIdType.MESH
 
 X_UP = [i for i in range(19) if DIRS[i][0] == 1]
@@ -131,7 +132,7 @@
     def at(d_plate, d_sub):
         return (lax.rem(plate + d_plate + n_plate, n_plate), lax.rem(me + d_sub + n_sub, n_sub))
 
-    targets = [(1, 0), (-1, 0), (0, 1), (0, -1)] + [DIRS[i][:2] for i in EDGES]
+    targets = [(1, 0), (-1, 0), (0, 1), (0, -1)]
     greeted = {(0, k) for k in range(1, n_sub)}
     greeted |= {(a % n_plate, b % n_sub) for a, b in targets}
     greeted = sorted(greeted)
@@ -198,6 +199,19 @@
                 device_id_type=MESH,
             ).wait_recv()
 
+    def remote(step, n, src, dst, offsets):
+        copy = pltpu.make_async_remote_copy(
+            src_ref=src,
+            dst_ref=dst,
+            send_sem=halo_s.at[step, n],
+            recv_sem=halo_r.at[step, n],
+            device_id=at(*offsets),
+            device_id_type=MESH,
+        )
+        copy.start()
+        return copy
+
+    ends = [[i for i in EDGES if DIRS[i][0] == sign] for sign in (1, -1)]
     sent = to_all(marks, mark_s, mark_r)
 
     def moments(pops):
@@ -219,8 +233,8 @@
     for load in loads[5:]:
         load.wait()
     fluid = solid_ref[...] == 0
+    mask = jnp.where(fluid, 1.0, 0.0)
     keep = 1.0 - 1.0 / RELAX
-    row = lax.broadcasted_iota(jnp.int32, (nx, ny, nz), 1)
     disp = None
     for step in range(STEPS):
         source = pops_ref if step == 0 else mid
@@ -246,7 +260,18 @@
                 for k in range(4):
                     w = jnp.where(x_first == x - k, x_w[k], w)
                 planes.append(w * y_rows)
+            outside = []
+            for y in (lax.rem(me + n_sub - 1, n_sub) * ny + ny - 1, lax.rem(me + 1, n_sub) * ny):
+                y_row = jnp.zeros_like(y_w[0])
+                for k in range(4):
+                    y_row = jnp.where(corners[1:2] == y - k, y_w[k], y_row)
+                for x in range(nx):
+                    w = jnp.zeros_like(x_w[0])
+                    for k in range(4):
+                        w = jnp.where(x_first == x - k, x_w[k], w)
+                    outside.append(w * y_row)
             xy_rows = jnp.concatenate(planes, 0)
+            xy_outside = jnp.concatenate(outside, 0)
             z_rows = split(dense_rows(corners[2:3], z_w, nz))
             target = [first[3 + k : 4 + k] for k in range(3)]
             spring = first[6:7]
@@ -274,6 +299,15 @@
             post[step, SLOT[i]] = jnp.where(fluid, keep * a + (even + odd), b)
             post[step, SLOT[j]] = jnp.where(fluid, keep * b + (even - odd), a)
 
+        for side, (names, y) in enumerate(((Y_UP, ny - 1), (Y_DN, 0))):
+            for n, i in enumerate(names):
+                y_send[step, side, n] = post[step, SLOT[i], :, y : y + 1, :]
+            y_send[step, side, len(names)] = mask[:, y : y + 1, :]
+        early = [
+            remote(step, 2 + side, y_send.at[step, side], y_recv.at[step, side], targets[2 + side])
+            for side in range(2)
+        ]
+
         all_here(velsum.at[step], vel_s.at[step], vel_r.at[step])
         summed = velsum[step, 0]
         for s in range(1, n_sub):
@@ -281,41 +315,37 @@
         moved = [summed[:, k * total : (k + 1) * total] for k in range(3)]
         force = [KAPPA * (target[k] - moved[k]) - spring * disp[k] for k in range(3)]
         disp = [disp[k] + moved[k] for k in range(3)]
-        weighted = split(jnp.concatenate([xy_rows * force[k] for k in range(3)], 0))
-        spread = dot3(weighted, z_rows, ((1,), (1,))).reshape(3, nx, ny, nz)
+        rows = [xy_rows * force[k] for k in range(3)] + [xy_outside * force[k] for k in range(3)]
+        everywhere = dot3(split(jnp.concatenate(rows, 0)), z_rows, ((1,), (1,)))
+        spread = everywhere[: 3 * cells].reshape(3, nx, ny, nz)
+        beyond = everywhere[3 * cells :].reshape(3, 2, nx, 1, nz)
         spread = [jnp.where(fluid, spread[k], 0.0) for k in range(3)]
         for i, j in PAIRS:
             push = (3.0 * WEIGHTS[i]) * signed_sum(i, spread)
             post[step, SLOT[i]] = post[step, SLOT[i]] + push
             post[step, SLOT[j]] = post[step, SLOT[j]] - push
 
-        for n, i in enumerate(Y_UP):
-            y_send[step, 0, n] = post[step, SLOT[i], :, ny - 1 : ny, :]
-        for n, i in enumerate(Y_DN):
-            y_send[step, 1, n] = post[step, SLOT[i], :, 0:1, :]
-        for n, i in enumerate(EDGES):
-            x = nx - 1 if DIRS[i][0] == 1 else 0
-            y = ny - 1 if DIRS[i][1] == 1 else 0
-            e_send[step, n] = post[step, SLOT[i], x, y : y + 1, :]
-        ends = [
-            (post.at[step, pl.ds(0, len(X_UP)), nx - 1], x_recv.at[step, 0]),
-            (post.at[step, pl.ds(len(X_UP), len(X_DN)), 0], x_recv.at[step, 1]),
-            (y_send.at[step, 0], y_recv.at[step, 0]),
-            (y_send.at[step, 1], y_recv.at[step, 1]),
-        ] + [(e_send.at[step, n], e_recv.at[step, n]) for n in range(len(EDGES))]
-        halo = []
-        for n, ((src, dst), (a, b)) in enumerate(zip(ends, targets)):
-            copy = pltpu.make_async_remote_copy(
-                src_ref=src,
-                dst_ref=dst,
-                send_sem=halo_s.at[step, n],
-                recv_sem=halo_r.at[step, n],
-                device_id=at(a, b),
-                device_id_type=MESH,
+        halo = [
+            remote(step, 0, post.at[step, pl.ds(0, len(X_UP)), nx - 1], x_recv.at[step, 0], (1, 0)),
+            remote(
+                step, 1, post.at[step, pl.ds(len(X_UP), len(X_DN)), 0], x_recv.at[step, 1], (-1, 0)
+            ),
+        ]
+        for copy in early:
+            copy.wait_recv()
+        edges = {}
+        for side, names in enumerate((Y_UP, Y_DN)):
+            wet = y_recv[step, side, len(names)]
+            pushed = [beyond[k, side] * wet for k in range(3)]
+            for n, i in enumerate(names):
+                edges[i] = y_recv[step, side, n] + (3.0 * WEIGHTS[i]) * signed_sum(i, pushed)
+        for side, sign in enumerate((1, -1)):
+            for n, i in enumerate(ends[side]):
+                e_send[step, side, n] = edges[i][nx - 1 if sign == 1 else 0]
+            halo.append(
+                remote(step, 4 + side, e_send.at[step, side], e_recv.at[step, side], (sign, 0))
             )
-            copy.start()
-            halo.append(copy)
-        sent += halo
+        sent += early + halo
 
         dest = mid if step < STEPS - 1 else out_ref
         for i, (dx, dy, dz) in enumerate(DIRS):
@@ -339,14 +369,12 @@
                     face = pltpu.roll(face, dz % nz, 1)
                 dest[i, 0 if dx == 1 else nx - 1] = face
             if dy:
-                side, names = (0, Y_UP) if dy == 1 else (1, Y_DN)
-                edge = y_recv[step, side, names.index(i)]
-                if dx == 1:
-                    edge = jnp.concatenate(
-                        [e_recv[step, EDGES.index(i)][None], edge[: nx - 1]], 0
-                    )
-                elif dx == -1:
-                    edge = jnp.concatenate([edge[1:], e_recv[step, EDGES.index(i)][None]], 0)
+                edge = edges[i]
+                if dx:
+                    side = 0 if dx == 1 else 1
+                    corner = e_recv[step, side, ends[side].index(i)][None]
+                    parts = [corner, edge[: nx - 1]] if dx == 1 else [edge[1:], corner]
+                    edge = jnp.concatenate(parts, 0)
                 if dz:
                     edge = pltpu.roll(edge.reshape(nx, nz), dz % nz, 1).reshape(nx, 1, nz)
                 y = 0 if dy == 1 else ny - 1
@@ -364,6 +392,22 @@
         copy.wait_send()
 
 
+def write_out(pops, disp, force, pops_out, disp_out, force_out, sems):
+    count = pops.shape[0]
+    cuts = [count * k // PIECES for k in range(PIECES + 1)]
+    pairs = [(disp, disp_out), (force, force_out)]
+    for low, high in zip(cuts, cuts[1:]):
+        part = pl.ds(low, high - low)
+        pairs.append((pops.at[part], pops_out.at[part]))
+    copies = [
+        pltpu.make_async_copy(src, dst, sems.at[n]) for n, (src, dst) in enumerate(pairs)
+    ]
+    for copy in copies:
+        copy.start()
+    for copy in copies:
+        copy.wait()
+
+
 def shards(n_plate, n_sub, populations, solid, corner, frac, target, stiffness, displacement):
     _, nx, ny, nz = populations.shape
     count = stiffness.shape[0]
@@ -371,13 +415,14 @@
     vmem = pl.BlockSpec(memory_space=pltpu.VMEM)
     total = count * n_sub
     faces = len(X_UP)
-    return pl.pallas_call(
+    results = (
+        jax.ShapeDtypeStruct(populations.shape, f32),
+        jax.ShapeDtypeStruct(displacement.shape, f32),
+        jax.ShapeDtypeStruct(displacement.shape, f32),
+    )
+    values = pl.pallas_call(
         functools.partial(body, n_plate, n_sub),
-        out_shape=(
-            jax.ShapeDtypeStruct(populations.shape, f32),
-            jax.ShapeDtypeStruct(displacement.shape, f32),
-            jax.ShapeDtypeStruct(displacement.shape, f32),
-        ),
+        out_shape=results,
         in_specs=[pl.BlockSpec(memory_space=pltpu.HBM)] * 7,
         out_specs=(vmem,) * 3,
         scratch_shapes=[
@@ -393,23 +438,30 @@
             pltpu.VMEM((STEPS, 19, nx, ny, nz), f32),
             pltpu.VMEM((19, nx, ny, nz), f32),
             pltpu.VMEM((STEPS, 2, faces, ny, nz), f32),
-            pltpu.VMEM((STEPS, 2, faces, nx, 1, nz), f32),
-            pltpu.VMEM((STEPS, 2, faces, nx, 1, nz), f32),
-            pltpu.VMEM((STEPS, len(EDGES), 1, nz), f32),
-            pltpu.VMEM((STEPS, len(EDGES), 1, nz), f32),
+            pltpu.VMEM((STEPS, 2, faces + 1, nx, 1, nz), f32),
+            pltpu.VMEM((STEPS, 2, faces + 1, nx, 1, nz), f32),
+            pltpu.VMEM((STEPS, 2, len(EDGES) // 2, 1, nz), f32),
+            pltpu.VMEM((STEPS, 2, len(EDGES) // 2, 1, nz), f32),
             pltpu.VMEM((8, 2 * count), f32),
             pltpu.SemaphoreType.DMA((n_sub,)),
             pltpu.SemaphoreType.DMA((n_sub,)),
             pltpu.SemaphoreType.DMA((STEPS, n_sub)),
             pltpu.SemaphoreType.DMA((STEPS, n_sub)),
-            pltpu.SemaphoreType.DMA((STEPS, 8)),
-            pltpu.SemaphoreType.DMA((STEPS, 8)),
+            pltpu.SemaphoreType.DMA((STEPS, 6)),
+            pltpu.SemaphoreType.DMA((STEPS, 6)),
             pltpu.SemaphoreType.DMA((7,)),
         ],
         compiler_params=pltpu.CompilerParams(
             collective_id=0, has_side_effects=True, vmem_limit_bytes=62 * 1024 * 1024
         ),
     )(populations, solid, corner, frac, target, stiffness[None], displacement)
+    return pl.pallas_call(
+        write_out,
+        out_shape=results,
+        in_specs=[vmem] * 3,
+        out_specs=(pl.BlockSpec(memory_space=pltpu.HBM),) * 3,
+        scratch_shapes=[pltpu.SemaphoreType.DMA((PIECES + 2,))],
+    )(*values)
 
 
 def solution(mesh):

time: 33.4 us -> 31.4 us (0.940)
  local copies, waits for them, and re-layouts: 3.19 us -> 0 us
  Pallas kernels: 29.4 us -> 30.6 us
    unnamed x7 -> x0, local copies, waits for them, and re-layouts: 3.19 us -> none
    pallas_call x1 -> x2, Pallas kernels: 29.4 us -> 30.6 us  [the longest x1 28.7 us: shards(): pl.pallas_call(functools.partial(body, n_plate, n_sub), out_shape=results...]
where the time goes in v3:
time: 31.4 us; the launch traced here: 31.3 us
  Pallas kernels  30.6 us (97%)
  between operations  0.64 us (2%)
    pallas_call x1, Pallas kernels, shards(): pl.pallas_call(functools.partial(body, n_plate, n_sub), out_shape=results...  28.7 us
    pallas_call x1, Pallas kernels, shards(): pl.pallas_call(write_out, out_shape=results, in_specs=[vmem] * 3, out_spe...  1.96 us

profile of v3, /device:TPU:0, one launch (start us, length us, event | category | flops | bytes accessed | tf_op | source)
XLA Modules:
  0.0 31.3 jit_solution(16262615845111816235)
XLA Ops:
  0.6 28.7 %shard_map.94 = (f32[19,4,16,128]{3,2,1,0:T(8,128)}, f32[3,64]{1,0:T(4,128)}, f32[3,64]{1,0:T(4,128)}) custom-call(f32[19,4,16,128]{3,2,1,0:T(8,128)} %pops_hbm.1, s32[4,16,128]{2,1,0:T(8,128)} %solid_hbm.1, s32[3,64]{1,0:T(4,128)} %corner_hbm.1, f32[3,64]{1,0:T(4,128)} %frac_hbm.1, f32[3,64]{1,0:T(4,128)} %target_hbm.1, f32[1,64]{1,0:T(1,128)} %bitcast.1, ...), custom_call_target="tpu_custom_call" | custom-call | tf_op jit(solution)/shard_map/pallas_call | solution.py:423
  29.3 2.0 %shard_map.95 = (f32[19,4,16,128]{3,2,1,0:T(8,128)}, f32[3,64]{1,0:T(4,128)}, f32[3,64]{1,0:T(4,128)}) custom-call(f32[19,4,16,128]{3,2,1,0:T(8,128)} %get-tuple-element.6.pops, f32[3,64]{1,0:T(4,128)} %get-tuple-element.7.disp, f32[3,64]{1,0:T(4,128)} %get-tuple-element.8.force), custom_call_target="tpu_custom_call" | custom-call | tf_op jit(solution)/shard_map/pallas_call | solution.py:458
